TPU v7x, 32 devices: a whole 2x2x4 slice. The times are simulated.
32 devices in a mesh: seq: 8 (over z, x), head: 4 (over y, core).
Axes of the slice: x: 2, y: 2, z: 4, core: 2. Of those that a mesh axis runs over, the one named last changes fastest.
Arguments:
- query_in: bfloat16 [4096, 256], P('seq', 'head'), may hold values from -6 to 6
- key_in: bfloat16 [4096, 256], P('seq', 'head'), may hold values from -6 to 6
- value_in: bfloat16 [4096, 2048], P('seq', 'head'), may hold values from -8 to 8
- conv_query: float32 [3, 256], P(None, 'head'), may hold values from -3.5 to 3.5
- conv_key: float32 [3, 256], P(None, 'head'), may hold values from -3.5 to 3.5
- conv_value: float32 [3, 2048], P(None, 'head'), may hold values from -3.5 to 3.5
- out_proj: bfloat16 [2048, 2048], P('head'), may hold values from -0.125 to 0.125
- out_grad: bfloat16 [4096, 2048], P(('seq', 'head')), may hold values from -8 to 8
Outputs:
- mixed: bfloat16 [4096, 2048], P(('seq', 'head'))
- grad_query: float32 [4096, 256], P('seq', 'head')
- grad_key: float32 [4096, 256], P('seq', 'head')
- grad_value: float32 [4096, 2048], P('seq', 'head')
- grad_conv_query: float32 [3, 256], P(None, 'head')
- grad_conv_key: float32 [3, 256], P(None, 'head')
- grad_conv_value: float32 [3, 2048], P(None, 'head')
All inputs are finite; a program needn't handle non-finite values.
Results may differ from a plain program's by a relative error of at most 0.0049.
Values may be sent and summed in bfloat16 or wider, within the bound.
A program may use at most 192 MiB of HBM per device.

v0:
```python
import functools
import math

import jax
import jax.numpy as jnp
import ml_dtypes
import numpy as np
from jax import lax
from jax.experimental import pallas as pl
from jax.experimental.pallas import tpu as pltpu
from jax.sharding import PartitionSpec as P

VD = 128
LANES = 128
RIM = 8
MESH = pl.DeviceIdType.MESH
F32, BF16 = jnp.float32, jnp.bfloat16
NN = (((1,), (0,)), ((), ()))
NT = (((1,), (1,)), ((), ()))
TN = (((0,), (0,)), ((), ()))


def round_up(number, step):
    return (number + step - 1) // step * step


def feature_tables(fk, heads):
    feat = fk * (fk + 1) // 2 + fk + 1
    lanes = round_up(feat, LANES)
    pick_a = np.zeros((heads, heads * fk, lanes), np.float32)
    pick_b = np.zeros((heads, heads * fk, lanes), np.float32)
    rows = np.zeros((8, lanes), np.float32)
    column = 0
    for i in range(fk):
        for j in range(i, fk):
            for h in range(heads):
                pick_a[h, h * fk + i, column] = 1.0
                pick_b[h, h * fk + j, column] = 1.0
            rows[2, column] = 1.0 / math.sqrt(2.0 * fk if i == j else fk)
            column += 1
    for i in range(fk):
        for h in range(heads):
            pick_a[h, h * fk + i, column] = 1.0
        rows[1, column] = 1.0
        rows[2, column] = fk ** -0.25
        column += 1
    rows[0, column] = rows[1, column] = rows[2, column] = 1.0
    mask = np.zeros((heads, 8, heads * fk), np.float32)
    for h in range(heads):
        mask[h, :, h * fk : (h + 1) * fk] = 1.0
    return pick_a.astype(ml_dtypes.bfloat16), pick_b.astype(ml_dtypes.bfloat16), rows, mask, feat


def dot(a, b, dims):
    return lax.dot_general(a, b, dims, preferred_element_type=F32)


def split(x):
    high = x.astype(BF16)
    return high, (x - high.astype(F32)).astype(BF16)


def dot3(a, b, dims):
    return dot(a[0], b[0], dims) + dot(a[0], b[1], dims) + dot(a[1], b[0], dims)


def kernel(n_seq, n_head, fk, feat_rows,
           q_ref, k_ref, v_ref, cq_ref, ck_ref, cv_ref, w_ref, og_ref,
           pa_ref, pb_ref, rows_ref, mask_ref,
           mixed_ref, gq_ref, gk_ref, gv_ref, gcq_ref, gck_ref, gcv_ref,
           ext, gcon, qs, ks, vs, pq, pk, dsim, wh, wl, num, den, up, dgr, att, gvs,
           og_all, m_send, m_recv, m_own,
           tf, rf, pf, tb, rb, pb, tt, tr,
           halo_sem, og_sem, m_sem, f_sem, b_sem, t_sem):
    T, HK = q_ref.shape
    VC = v_ref.shape[1]
    H = VC // VD
    CW = ext.shape[1]
    FP = feat_rows
    FL = pa_ref.shape[2]
    TS = T // n_head
    bits = [1 << i for i in range(n_seq.bit_length() - 1)]
    L = len(bits)
    s = lax.axis_index("seq")
    h_me = lax.axis_index("head")

    def flip(index, b):
        return index + b - 2 * b * ((index // b) % 2)

    def flip_all(index, r):
        b = 1
        while b <= r:
            if r & b:
                index = flip(index, b)
            b *= 2
        return index

    nxt = (s + 1) % n_seq
    prv = (s + n_seq - 1) % n_seq

    barrier = pltpu.get_barrier_semaphore()
    for b in bits:
        pl.semaphore_signal(barrier, inc=1, device_id={"seq": flip(s, b)}, device_id_type=MESH)
    for other in (nxt, prv):
        pl.semaphore_signal(barrier, inc=1, device_id={"seq": other}, device_id_type=MESH)
    for r in range(1, n_head):
        pl.semaphore_signal(barrier, inc=1, device_id={"head": flip_all(h_me, r)}, device_id_type=MESH)

    zero_pad = jnp.zeros((T, LANES - HK), F32)
    ext[RIM:, 0:LANES] = jnp.concatenate([q_ref[...].astype(F32), zero_pad], axis=1)
    ext[RIM:, LANES : 2 * LANES] = jnp.concatenate([k_ref[...].astype(F32), zero_pad], axis=1)
    ext[RIM:, 2 * LANES :] = v_ref[...].astype(F32)

    pl.semaphore_wait(barrier, L + 2 + n_head - 1)

    def remote(src, dst, sem, where):
        return pltpu.make_async_remote_copy(
            src_ref=src, dst_ref=dst, send_sem=sem[0], recv_sem=sem[1],
            device_id=where, device_id_type=MESH)

    halo = remote(ext.at[pl.ds(T, RIM)], ext.at[pl.ds(0, RIM)],
                  (halo_sem.at[0, 0], halo_sem.at[0, 1]), {"seq": nxt})
    halo.start()

    head_bits = [1 << i for i in reversed(range(n_head.bit_length() - 1))]
    og_copies = {}
    held = [0]
    for b in head_bits:
        for r in held:
            src = og_ref if r == 0 else og_all.at[r]
            og_copies[r ^ b] = (r, remote(src, og_all.at[r ^ b],
                                          (og_sem.at[r ^ b, 0], og_sem.at[r ^ b, 1]),
                                          {"head": flip(h_me, b)}))
        held = held + [r ^ b for r in held]
    for r, (src, copy) in og_copies.items():
        if src == 0:
            copy.start()

    def tap_row(j):
        pad = jnp.zeros((1, LANES - HK), F32)
        return jnp.concatenate(
            [cq_ref[j : j + 1, :], pad, ck_ref[j : j + 1, :], pad, cv_ref[j : j + 1, :]], axis=1)

    taps = [tap_row(j) for j in range(3)]

    halo.wait_recv()
    ext[0:RIM, :] = jnp.where(s == 0, 0.0, ext[0:RIM, :])

    def conv(lo, hi):
        total = taps[0][:, lo:hi] * ext[RIM : RIM + T, lo:hi]
        total = total + taps[1][:, lo:hi] * ext[RIM - 1 : RIM - 1 + T, lo:hi]
        return total + taps[2][:, lo:hi] * ext[RIM - 2 : RIM - 2 + T, lo:hi]

    qs[...] = conv(0, LANES)[:, :HK]
    ks[...] = conv(LANES, 2 * LANES)[:, :HK]
    for h in range(H):
        vs[h] = conv((2 + h) * LANES, (3 + h) * LANES)

    row_a = rows_ref[0:1, :]
    row_b = rows_ref[1:2, :]
    row_c = rows_ref[2:3, :]

    def factors(x, h):
        high, low = split(x)
        a = dot(high, pa_ref[h], NN) + dot(low, pa_ref[h], NN)
        b = dot(high, pb_ref[h], NN) + dot(low, pb_ref[h], NN)
        return (a + row_a) * row_c, b + row_b

    def pull(x, dphi, h):
        a, b = factors(x, h)
        left = split(dphi * b * row_c)
        right = split(dphi * a)
        return (dot(left[0], pa_ref[h], NT) + dot(left[1], pa_ref[h], NT)
                + dot(right[0], pb_ref[h], NT) + dot(right[1], pb_ref[h], NT))

    def put_state(buf, h, state, total):
        buf[0, h, 0:FP, :] = state
        for c in range(FL // LANES):
            buf[0, h, FP + c : FP + c + 1, :] = total[:, c * LANES : (c + 1) * LANES]

    def sums_of(buf, h):
        return jnp.concatenate(
            [buf[h, FP + c : FP + c + 1, :] for c in range(FL // LANES)], axis=1)

    def hop(send, recv, sem, l, h):
        return remote(send.at[l, h], recv.at[l, h], (sem.at[l, h, 0], sem.at[l, h, 1]),
                      {"seq": flip(s, bits[l])})

    def stage(send, recv, total, sem, l, later):
        bit = (s // bits[l]) % 2
        wanted = bit == (0 if later else 1)

        def one(h, _):
            hop(send, recv, sem, l, h).wait_recv()
            arrived = recv[l, h]
            mine = jnp.where(wanted, arrived, 0.0)
            total[h] = mine if l == 0 else total[h] + mine
            if l + 1 < L:
                send[l + 1, h] = send[l, h] + arrived
                hop(send, recv, sem, l + 1, h).start()
            return 0

        lax.fori_loop(0, H, one, 0)

    def key_side(h, _):
        a, b = factors(ks[...], h)
        phi = a * b
        pk[h] = phi
        state = dot3(split(phi[:, :FP]), split(vs[h]), TN)
        put_state(tf, h, state, jnp.sum(phi, axis=0, keepdims=True))
        hop(tf, rf, f_sem, 0, h).start()
        return 0

    for l in range(L):
        for h in range(H):
            for buf in (tf, tb):
                buf[l, h, FP:, :] = jnp.zeros((buf.shape[2] - FP, LANES), F32)
    lax.fori_loop(0, H, key_side, 0)

    def query_side(h, _):
        x = qs[...]
        a, b = factors(x, h)
        pq[h] = a * b
        sim = dot3(split(x * mask_ref[h, 0:1, :]), split(ks[...]), NT) * fk ** -0.5
        causal = (lax.broadcasted_iota(jnp.int32, (T, T), 0)
                  >= lax.broadcasted_iota(jnp.int32, (T, T), 1))
        weights = jnp.where(causal, 1.0 + sim + 0.5 * sim * sim, 0.0)
        dsim[h] = jnp.where(causal, (1.0 + sim) * fk ** -0.5, 0.0)
        high, low = split(weights)
        wh[h] = high
        wl[h] = low
        den[h] = jnp.sum(weights, axis=1, keepdims=True)
        return 0

    lax.fori_loop(0, H, query_side, 0)

    stage(tf, rf, pf, f_sem, 0, False)

    for r, (src, copy) in og_copies.items():
        if src != 0:
            og_copies[src][1].wait_recv()
            copy.start()

    def numer_side(h, _):
        num[h] = dot3((wh[h], wl[h]), split(vs[h]), NN)
        return 0

    lax.fori_loop(0, H, numer_side, 0)
    if L > 1:
        stage(tf, rf, pf, f_sem, 1, False)

    forwarded = {src for src, _ in og_copies.values() if src != 0}
    for r in held:
        if r != 0 and r not in forwarded:
            og_copies[r][1].wait_recv()
        block = og_ref[...] if r == 0 else og_all[r]
        first = pl.multiple_of(flip_all(h_me, r) * TS, TS)
        product = dot(block, w_ref[...], NT)
        for h in range(H):
            up[h, pl.ds(first, TS), :] = product[:, h * VD : (h + 1) * VD]

    for l in range(2, L):
        stage(tf, rf, pf, f_sem, l, False)

    def attend(h, _):
        phi = pq[h]
        denom = den[h] + jnp.sum(phi * sums_of(pf, h), axis=1, keepdims=True)
        phi_s = split(phi[:, :FP])
        numer = num[h] + dot3(phi_s, split(pf[h, 0:FP, :]), NN)
        inv = 1.0 / denom
        out = numer * inv
        att[h] = out.astype(BF16)
        upstream = up[h]
        g = upstream * inv
        up[h] = g
        dg = -jnp.sum(upstream * out, axis=1, keepdims=True) * inv
        dgr[h] = dg
        put_state(tb, h, dot3(phi_s, split(g), TN), jnp.sum(phi * dg, axis=0, keepdims=True))
        hop(tb, rb, b_sem, 0, h).start()
        return 0

    lax.fori_loop(0, H, attend, 0)

    def m_copy(r):
        return remote(m_send.at[r], m_recv.at[r], (m_sem.at[r, 0], m_sem.at[r, 1]),
                      {"head": flip_all(h_me, r)})

    for r in sorted(range(n_head), reverse=True):
        first = pl.multiple_of(flip_all(h_me, r) * TS, TS)
        block = jnp.concatenate([att[h, pl.ds(first, TS), :] for h in range(H)], axis=1)
        part = dot(block, w_ref[...], NN)
        if r:
            m_send[r] = part.astype(BF16)
            m_copy(r).start()
        else:
            m_own[...] = part

    stage(tb, rb, pb, b_sem, 0, True)

    gcon[0:T, 0 : 2 * LANES] = jnp.zeros((T, 2 * LANES), F32)

    def query_grads(h, _):
        g = split(up[h])
        dg = dgr[h]
        dphi = dot3(g, split(pf[h, 0:FP, :]), NT)
        dphi = jnp.concatenate([dphi, jnp.zeros((T, FL - FP), F32)], axis=1) + dg * sums_of(pf, h)
        ds = split((dot3(g, split(vs[h]), NT) + dg) * dsim[h])
        mask = mask_ref[h, 0:1, :]
        gcon[0:T, 0:HK] = (gcon[0:T, 0:HK] + pull(qs[...], dphi, h)
                           + dot3(ds, split(ks[...]), NN) * mask)
        gcon[0:T, LANES : LANES + HK] = (gcon[0:T, LANES : LANES + HK]
                                         + dot3(ds, split(qs[...]), TN) * mask)
        return 0

    lax.fori_loop(0, H, query_grads, 0)
    if L > 1:
        stage(tb, rb, pb, b_sem, 1, True)

    def value_local(h, _):
        gvs[h] = dot3((wh[h], wl[h]), split(up[h]), TN)
        return 0

    lax.fori_loop(0, H, value_local, 0)
    for l in range(2, L):
        stage(tb, rb, pb, b_sem, l, True)

    def key_grads(h, _):
        later = split(pb[h, 0:FP, :])
        dphi = dot3(split(vs[h]), later, NT)
        dphi = jnp.concatenate([dphi, jnp.zeros((T, FL - FP), F32)], axis=1) + sums_of(pb, h)
        gcon[0:T, LANES : LANES + HK] = gcon[0:T, LANES : LANES + HK] + pull(ks[...], dphi, h)
        gvs[h] = gvs[h] + dot3(split(pk[h][:, :FP]), later, NN)
        return 0

    lax.fori_loop(0, H, key_grads, 0)
    for h in range(H):
        gcon[0:T, (2 + h) * LANES : (3 + h) * LANES] = gvs[h]

    tail = remote(gcon.at[pl.ds(0, RIM)], gcon.at[pl.ds(T, RIM)],
                  (halo_sem.at[1, 0], halo_sem.at[1, 1]), {"seq": prv})
    tail.start()

    def t_hop(l):
        return remote(tt.at[l], tr.at[l], (t_sem.at[l, 0], t_sem.at[l, 1]), {"seq": flip(s, bits[l])})

    grads = gcon[0:T, :]
    tt[0, 0:8, :] = jnp.concatenate(
        [jnp.sum(grads * ext[RIM - j : RIM - j + T, :], axis=0, keepdims=True) for j in range(3)]
        + [jnp.zeros((5, CW), F32)], axis=0)
    t_hop(0).start()

    tail.wait_recv()
    gcon[T : T + RIM, :] = jnp.where(s == n_seq - 1, 0.0, gcon[T : T + RIM, :])

    def conv_back(lo, hi):
        return (taps[0][:, lo:hi] * gcon[0:T, lo:hi] + taps[1][:, lo:hi] * gcon[1 : T + 1, lo:hi]
                + taps[2][:, lo:hi] * gcon[2 : T + 2, lo:hi])

    def t_stage(l):
        t_hop(l).wait_recv()
        tt[l + 1] = tt[l] + tr[l]
        if l + 1 < L:
            t_hop(l + 1).start()

    gq_ref[...] = conv_back(0, LANES)[:, :HK]
    gk_ref[...] = conv_back(LANES, 2 * LANES)[:, :HK]
    t_stage(0)
    gv_ref[...] = conv_back(2 * LANES, CW)
    if L > 1:
        t_stage(1)
    total = m_own[...]
    for r in range(1, n_head):
        m_copy(r).wait_recv()
        total = total + m_recv[r].astype(F32)
    mixed_ref[...] = total.astype(BF16)
    for l in range(2, L):
        t_stage(l)
    gcq_ref[...] = tt[L, 0:3, 0:HK]
    gck_ref[...] = tt[L, 0:3, LANES : LANES + HK]
    gcv_ref[...] = tt[L, 0:3, 2 * LANES :]

    halo.wait_send()
    tail.wait_send()
    for _, copy in og_copies.values():
        copy.wait_send()
    for r in range(1, n_head):
        m_copy(r).wait_send()
    for l in range(L):
        t_hop(l).wait_send()

        def drain(h, _):
            hop(tf, rf, f_sem, l, h).wait_send()
            hop(tb, rb, b_sem, l, h).wait_send()
            return 0

        lax.fori_loop(0, H, drain, 0)


def solution(mesh):
    n_seq, n_head = mesh.shape["seq"], mesh.shape["head"]

    def body(query_in, key_in, value_in, conv_query, conv_key, conv_value, out_proj, out_grad):
        T, HK = query_in.shape
        VC = value_in.shape[1]
        D = out_proj.shape[1]
        H = VC // VD
        fk = HK // H
        pick_a, pick_b, rows, mask, feat = feature_tables(fk, H)
        FL = rows.shape[1]
        FP = round_up(feat, 8)
        FS = FP + 8
        CW = 2 * LANES + VC
        L = n_seq.bit_length() - 1
        TS = T // n_head
        vmem = pl.BlockSpec(memory_space=pltpu.VMEM)
        shape = jax.ShapeDtypeStruct
        big = pltpu.VMEM
        dma = pltpu.SemaphoreType.DMA
        return pl.pallas_call(
            functools.partial(kernel, n_seq, n_head, fk, FP),
            out_shape=(
                shape((TS, D), BF16), shape((T, HK), F32), shape((T, HK), F32), shape((T, VC), F32),
                shape((3, HK), F32), shape((3, HK), F32), shape((3, VC), F32),
            ),
            in_specs=[vmem] * 12,
            out_specs=tuple([vmem] * 7),
            scratch_shapes=[
                big((RIM + T, CW), F32), big((T + RIM, CW), F32),
                big((T, HK), F32), big((T, HK), F32), big((H, T, VD), F32),
                big((H, T, FL), F32), big((H, T, FL), F32),
                big((H, T, T), F32), big((H, T, T), BF16), big((H, T, T), BF16),
                big((H, T, VD), F32), big((H, T, 1), F32), big((H, T, VD), F32),
                big((H, T, 1), F32), big((H, T, VD), BF16), big((H, T, VD), F32),
                big((n_head, TS, D), BF16), big((n_head, TS, D), BF16),
                big((n_head, TS, D), BF16), big((TS, D), F32),
                big((L, H, FS, VD), F32), big((L, H, FS, VD), F32), big((H, FS, VD), F32),
                big((L, H, FS, VD), F32), big((L, H, FS, VD), F32), big((H, FS, VD), F32),
                big((L + 1, 8, CW), F32), big((L, 8, CW), F32),
                dma((2, 2)), dma((n_head, 2)), dma((n_head, 2)),
                dma((L, H, 2)), dma((L, H, 2)), dma((L, 2)),
            ],
            compiler_params=pltpu.CompilerParams(
                collective_id=0, has_side_effects=True, vmem_limit_bytes=58 * 1024 * 1024),
        )(query_in, key_in, value_in, conv_query, conv_key, conv_value, out_proj, out_grad,
          jnp.asarray(pick_a), jnp.asarray(pick_b), jnp.asarray(rows), jnp.asarray(mask))

    in_specs = (
        P("seq", "head"), P("seq", "head"), P("seq", "head"),
        P(None, "head"), P(None, "head"), P(None, "head"),
        P("head", None), P(("seq", "head"), None),
    )
    out_specs = (
        P(("seq", "head"), None), P("seq", "head"), P("seq", "head"), P("seq", "head"),
        P(None, "head"), P(None, "head"), P(None, "head"),
    )
    return jax.shard_map(body, mesh=mesh, in_specs=in_specs, out_specs=out_specs, check_vma=False)
```

profile of v0, /device:TPU:24, one launch (start us, length us, event | category | flops | bytes accessed | tf_op | source)
XLA Modules:
  0.0 94.4 jit_solution(12314507567605898860)
XLA Ops:
  0.6 1.6 %copy.19.q_ref = bf16[512,64]{1,0:T(8,128)(2,1)} copy(bf16[512,64]{0,1:T(8,128)(2,1)} %param.12) | data formatting | bytes 131072 | tf_op args[0]
  2.2 1.6 %copy.20.k_ref = bf16[512,64]{1,0:T(8,128)(2,1)} copy(bf16[512,64]{0,1:T(8,128)(2,1)} %param.13) | data formatting | bytes 131072 | tf_op args[1]
  3.8 82.3 %shard_map.171 = (bf16[128,2048]{1,0:T(8,128)(2,1)}, f32[512,64]{1,0:T(8,128)}, f32[512,64]{1,0:T(8,128)}, f32[512,512]{1,0:T(8,128)}, f32[3,64]{1,0:T(4,128)}, /*index=5*/f32[3,64]{1,0:T(4,128)}, f32[3,512]{1,0:T(4,128)}) custom-call(bf16[512,64]{1,0:T(8,128)(2,1)} %copy.19.q_ref, bf16[512,64]{1,0:T(8,128)(2,1)} %copy.20.k_ref, bf16[512,512]{1,0:T(8,128)(2,1)} %v_ref.1, ...), custom_call_target="tpu_custom_call" | custom-call | tf_op jit(solution)/shard_map/pallas_call | solution.py:419
  86.2 0.0 copy-start
  86.2 0.0 copy-start.3
  86.2 0.0 copy-start.2
  86.2 0.0 copy-start.1
  86.2 1.8 %copy.21 = f32[512,64]{0,1:T(8,128)} copy(f32[512,64]{1,0:T(8,128)} %get-tuple-element.8) | data formatting | bytes 262144 | tf_op jit(solution)/shard_map/pallas_call | solution.py:419
  88.0 1.7 %copy.22 = f32[512,64]{0,1:T(8,128)} copy(f32[512,64]{1,0:T(8,128)} %get-tuple-element.9) | data formatting | bytes 262144 | tf_op jit(solution)/shard_map/pallas_call | solution.py:419
  89.7 1.9 %copy.28 = bf16[128,2048]{1,0:T(8,128)(2,1)} copy(bf16[128,2048]{1,0:T(8,128)(2,1)} %get-tuple-element.21) | data formatting | bytes 1048576
  91.6 0.0 copy-done
  91.6 1.0 %copy.29 = f32[512,512]{1,0:T(8,128)} copy(f32[512,512]{1,0:T(8,128)S(1)} %copy-done) | data formatting | bytes 2097152
  92.6 0.0 copy-done.3
  92.6 0.6 copy.30
  93.2 0.0 copy-done.2
  93.2 0.6 copy.31
  93.8 0.0 copy-done.1
  93.8 0.6 copy.32
Async XLA Ops:
  86.2 5.4 %copy-start = (f32[512,512]{1,0:T(8,128)S(1)}, f32[512,512]{1,0:T(8,128)}, u32[]{:S(2)}) copy-start(f32[512,512]{1,0:T(8,128)} %get-tuple-element.24) | copy-start | bytes 3145732
  86.2 6.4 %copy-start.3 = (f32[3,64]{1,0:T(4,128)S(1)}, f32[3,64]{1,0:T(4,128)}, u32[]{:S(2)}) copy-start(f32[3,64]{1,0:T(4,128)} %get-tuple-element.25) | copy-start | bytes 2308
  86.2 7.0 %copy-start.2 = (f32[3,64]{1,0:T(4,128)S(1)}, f32[3,64]{1,0:T(4,128)}, u32[]{:S(2)}) copy-start(f32[3,64]{1,0:T(4,128)} %get-tuple-element.26) | copy-start | bytes 2308
  86.2 7.6 %copy-start.1 = (f32[3,512]{1,0:T(4,128)S(1)}, f32[3,512]{1,0:T(4,128)}, u32[]{:S(2)}) copy-start(f32[3,512]{1,0:T(4,128)} %get-tuple-element.27) | copy-start | bytes 18436
where the time goes:
time: 96.3 us; the launch traced here: 94.4 us
  Pallas kernels  82.3 us (85%)
  local copies, waits for them, and re-layouts  11.3 us (12%)
    pallas_call x1, Pallas kernels, body(): pl.pallas_call(functools.partial(kernel, n_seq, n_head, fk, FP), out_shap...  82.3 us
    unnamed x15, local copies, waits for them, and re-layouts  7.82 us
    pallas_call x2, local copies, waits for them, and re-layouts, body(): pl.pallas_call(functools.partial(kernel, n_seq, n_head, fk, FP), out_shap...  3.53 us

commit v1 on v0

v1 whole, which is shorter than its diff:
```python
import functools
import math

import jax
import jax.numpy as jnp
import ml_dtypes
import numpy as np
from jax import lax
from jax.experimental import pallas as pl
from jax.experimental.pallas import tpu as pltpu
from jax.sharding import PartitionSpec as P

VD = 128
LANES = 128
RIM = 8
MESH = pl.DeviceIdType.MESH
F32, BF16 = jnp.float32, jnp.bfloat16
NN = (((1,), (0,)), ((), ()))
NT = (((1,), (1,)), ((), ()))
TN = (((0,), (0,)), ((), ()))


def round_up(number, step):
    return (number + step - 1) // step * step


def feature_tables(fk, heads):
    feat = fk * (fk + 1) // 2 + fk + 1
    lanes = round_up(feat, LANES)
    pick = np.zeros((heads, 2, heads * fk, 2 * lanes), np.float32)
    rows = np.zeros((8, lanes), np.float32)
    column = 0
    for i in range(fk):
        for j in range(i, fk):
            for h in range(heads):
                pick[h, :, h * fk + i, column] = 1.0
                pick[h, :, h * fk + j, lanes + column] = 1.0
            rows[2, column] = 1.0 / math.sqrt(2.0 * fk if i == j else fk)
            column += 1
    for i in range(fk):
        for h in range(heads):
            pick[h, :, h * fk + i, column] = 1.0
        rows[1, column] = 1.0
        rows[2, column] = fk ** -0.25
        column += 1
    rows[0, column] = rows[1, column] = rows[2, column] = 1.0
    mask = np.zeros((heads, 8, heads * fk), np.float32)
    for h in range(heads):
        mask[h, :, h * fk : (h + 1) * fk] = 1.0
    pick = pick.reshape(heads, 2 * heads * fk, 2 * lanes).astype(ml_dtypes.bfloat16)
    mask3 = np.concatenate([mask] * 3, axis=2).astype(ml_dtypes.bfloat16)
    return pick, rows, mask, np.concatenate([mask3, mask3], axis=1), feat


def dot(a, b, dims):
    return lax.dot_general(a, b, dims, preferred_element_type=F32)


def split(x):
    high = x.astype(BF16)
    return high, (x - high.astype(F32)).astype(BF16)


def beside(*parts):
    return jnp.concatenate(parts, axis=1)


def fold(x):
    half = x.shape[1] // 2
    return x[:, :half] + x[:, half:]


def kernel(n_seq, n_head, fk, feat, FP,
           q_ref, k_ref, v_ref, cq_ref, ck_ref, cv_ref, w_ref, og_ref,
           pick_ref, rows_ref, mask_ref, mask3_ref,
           mixed_ref, gq_ref, gk_ref, gv_ref, gcq_ref, gck_ref, gcv_ref,
           ext, gcon, q3, k3, q2, vcat, aq, bq, ak, bk, dsim, wh, ds_buf,
           num, den, up, gcat, dgr, att, gvs,
           og_all, m_send, m_recv, m_own,
           f_own, f_pair, f_send, f_chain, pf, b_own, b_pair, b_send, b_chain, pb,
           tr, tr_own,
           halo_sem, og_sem, m_sem, f_sem, b_sem, t_send, t_recv):
    HK, T = q_ref.shape
    VC = v_ref.shape[1]
    D = w_ref.shape[1]
    H = VC // VD
    CW = ext.shape[1]
    FL = rows_ref.shape[1]
    TS = T // n_head
    TB = math.gcd(T, 256)
    blocks = range(T // TB)
    Z = n_seq // 2
    s = lax.axis_index("seq")
    h_me = lax.axis_index("head")
    z, odd = s // 2, s % 2

    def flip_all(index, r):
        b = 1
        while b <= r:
            if r & b:
                index = index + b - 2 * b * ((index // b) % 2)
            b *= 2
        return index

    pair = s + 1 - 2 * odd
    nxt = (s + 1) % n_seq
    prv = (s + n_seq - 1) % n_seq

    barrier = pltpu.get_barrier_semaphore()

    def greet(d, _):
        pl.semaphore_signal(barrier, inc=1, device_id={"seq": (s + d) % n_seq}, device_id_type=MESH)
        return 0

    lax.fori_loop(1, n_seq, greet, 0)
    for r in range(1, n_head):
        pl.semaphore_signal(barrier, inc=1, device_id={"head": flip_all(h_me, r)}, device_id_type=MESH)

    zero_rows = jnp.zeros((LANES - HK, T), F32)
    ext[RIM:, 0:LANES] = jnp.concatenate([q_ref[...].astype(F32), zero_rows], axis=0).T
    ext[RIM:, LANES : 2 * LANES] = jnp.concatenate([k_ref[...].astype(F32), zero_rows], axis=0).T
    ext[RIM:, 2 * LANES :] = v_ref[...].astype(F32)

    pl.semaphore_wait(barrier, n_seq - 1 + n_head - 1)

    def remote(src, dst, sem, where):
        return pltpu.make_async_remote_copy(
            src_ref=src, dst_ref=dst, send_sem=sem[0], recv_sem=sem[1],
            device_id=where, device_id_type=MESH)

    halo = remote(ext.at[pl.ds(T, RIM)], ext.at[pl.ds(0, RIM)],
                  (halo_sem.at[0, 0], halo_sem.at[0, 1]), {"seq": nxt})
    halo.start()

    og_copies = {}
    held = [0]
    for b in [1 << i for i in reversed(range(n_head.bit_length() - 1))]:
        for r in held:
            src = og_ref if r == 0 else og_all.at[r]
            og_copies[r ^ b] = (r, remote(src, og_all.at[r ^ b],
                                          (og_sem.at[r ^ b, 0], og_sem.at[r ^ b, 1]),
                                          {"head": flip_all(h_me, b)}))
        held = held + [r ^ b for r in held]
    for r, (src, copy) in og_copies.items():
        if src == 0:
            copy.start()
    og_all[0] = og_ref[...]

    def tap_row(j):
        pad = jnp.zeros((1, LANES - HK), F32)
        return beside(cq_ref[j : j + 1, :], pad, ck_ref[j : j + 1, :], pad, cv_ref[j : j + 1, :])

    taps = [tap_row(j) for j in range(3)]
    row_a, row_b, row_c = (rows_ref[j : j + 1, :] for j in range(3))

    halo.wait_recv()
    ext[0:RIM, :] = jnp.where(s == 0, 0.0, ext[0:RIM, :])

    def conv(lo, hi):
        total = taps[0][:, lo:hi] * ext[RIM : RIM + T, lo:hi]
        total = total + taps[1][:, lo:hi] * ext[RIM - 1 : RIM - 1 + T, lo:hi]
        return total + taps[2][:, lo:hi] * ext[RIM - 2 : RIM - 2 + T, lo:hi]

    high, low = split(conv(LANES, 2 * LANES)[:, :HK])
    k3[...] = beside(high, low, high)
    for h in range(H):
        vcat[h] = beside(*split(conv((2 + h) * LANES, (3 + h) * LANES)))

    def put_state(buf, h, state, total):
        buf[h, :, :] = state
        for c in range(FL // LANES):
            buf[h, feat + c : feat + c + 1, :] = total[:, c * LANES : (c + 1) * LANES]

    def sums_of(buf, h):
        return beside(*[buf[h, feat + c : feat + c + 1, :] for c in range(FL // LANES)])

    def factors(x2, h, a_buf, b_buf):
        both = dot(x2, pick_ref[h], NN)
        a = (both[:, :FL] + row_a) * row_c
        b = both[:, FL:] + row_b
        a_buf[h] = a
        b_buf[h] = b
        return a * b

    def pull(dphi, h, a_buf, b_buf):
        both = beside((dphi * b_buf[h] * row_c).astype(BF16), (dphi * a_buf[h]).astype(BF16))
        return dot(both, pick_ref[h][:HK], NT)

    def to_state(phi, cat):
        high, low = split(phi[:, :FP])
        return fold(dot(high, cat, TN)) + dot(low, cat[:, :VD], TN)

    def by_state(phi, state):
        high, low = split(phi[:, :FP])
        st = beside(*split(state))
        return fold(dot(high, st, NN)) + dot(low, st[:, :VD], NN)

    def on_features(cat, state, total):
        high, low = split(state)
        dphi = dot(cat, beside(high, high), NT) + dot(cat[:, :VD], low, NT)
        return beside(dphi, jnp.zeros((T, FL - FP), F32)) + total

    class Scan:
        def __init__(self, own, pair_buf, send, chain, total, sem, later):
            self.own, self.pair_buf, self.send, self.chain = own, pair_buf, send, chain
            self.total, self.sem, self.later = total, sem, later
            self.place = Z - 1 - z if later else z
            self.wanted = odd == (0 if later else 1)
            self.target = (s + n_seq - 2) % n_seq if later else (s + 2) % n_seq

        def swap(self, h):
            return remote(self.own.at[h], self.pair_buf.at[h],
                          (self.sem.at[0, h, 0], self.sem.at[0, h, 1]), {"seq": pair})

        def pass_on(self, h):
            return remote(self.send.at[h], self.chain.at[h],
                          (self.sem.at[1, h, 0], self.sem.at[1, h, 1]), {"seq": self.target})

        def point(self, p):
            if p >= Z:
                return
            if p == 0:
                def one(h, _):
                    self.swap(h).wait_recv()
                    arrived = self.pair_buf[h]
                    self.total[h] = jnp.where(self.wanted, arrived, 0.0)
                    self.send[h] = self.own[h] + arrived
                    if Z > 1:
                        @pl.when(self.place == 0)
                        def _():
                            self.pass_on(h).start()
                    return 0

                lax.fori_loop(0, H, one, 0)
                return

            @pl.when(self.place == p if p < 3 else self.place >= p)
            def _():
                def one(h, _):
                    self.pass_on(h).wait_recv()
                    arrived = self.chain[h]

                    @pl.when(self.place < Z - 1)
                    def _():
                        self.send[h] = self.send[h] + arrived
                        self.pass_on(h).start()

                    self.total[h] = self.total[h] + arrived
                    return 0

                lax.fori_loop(0, H, one, 0)

        def drain(self):
            def one(h, _):
                self.swap(h).wait_send()

                @pl.when(self.place < Z - 1)
                def _():
                    self.pass_on(h).wait_send()

                return 0

            lax.fori_loop(0, H, one, 0)

    before = Scan(f_own, f_pair, f_send, f_chain, pf, f_sem, False)
    after = Scan(b_own, b_pair, b_send, b_chain, pb, b_sem, True)

    def key_side(h, _):
        phi = factors(k3[:, : 2 * HK], h, ak, bk)
        put_state(f_own, h, to_state(phi, vcat[h]), jnp.sum(phi, axis=0, keepdims=True))
        before.swap(h).start()
        return 0

    lax.fori_loop(0, H, key_side, 0)

    high, low = split(conv(0, LANES)[:, :HK])
    q3[...] = beside(high, high, low)
    q2[...] = beside(high, low)

    def query_side(h, _):
        factors(q2[...], h, aq, bq)
        mine = mask3_ref[h, 0:1, :]
        for i in blocks:
            rows, width = slice(i * TB, (i + 1) * TB), (i + 1) * TB
            sim = dot(q3[rows, :] * mine, k3[0:width, :], NT) * fk ** -0.5
            causal = (lax.broadcasted_iota(jnp.int32, (TB, width), 0) + i * TB
                      >= lax.broadcasted_iota(jnp.int32, (TB, width), 1))
            weights = jnp.where(causal, 1.0 + sim + 0.5 * sim * sim, 0.0).astype(BF16)
            dsim[h, rows, 0:width] = jnp.where(causal, (1.0 + sim) * fk ** -0.5, 0.0)
            wh[h, rows, 0:width] = weights
            den[h, rows, :] = jnp.sum(weights.astype(F32), axis=1, keepdims=True)
            num[h, rows, :] = fold(dot(weights, vcat[h, 0:width, :], NN))
        return 0

    cuts = [0, H // 2, H - H // 4, H]
    lax.fori_loop(cuts[0], cuts[1], query_side, 0)
    before.point(0)
    lax.fori_loop(cuts[1], cuts[2], query_side, 0)
    before.point(1)
    lax.fori_loop(cuts[2], cuts[3], query_side, 0)
    for r, (src, copy) in og_copies.items():
        if src != 0:
            og_copies[src][1].wait_recv()
            copy.start()
    before.point(2)

    forwarded = {src for src, _ in og_copies.values() if src != 0}
    for r in held:
        if r != 0 and r not in forwarded:
            og_copies[r][1].wait_recv()
    for h in range(H):
        product = dot(og_all[...].reshape(T, D), w_ref[h * VD : (h + 1) * VD, :], NT)
        for r in range(n_head):
            first = pl.multiple_of(flip_all(h_me, r) * TS, TS)
            up[h, pl.ds(first, TS), :] = product[r * TS : (r + 1) * TS]
    before.point(3)

    def attend(h, _):
        phi = aq[h] * bq[h]
        denom = den[h] + jnp.sum(phi * sums_of(pf, h), axis=1, keepdims=True)
        inv = 1.0 / denom
        out = (num[h] + by_state(phi, pf[h])) * inv
        att[h] = out.astype(BF16)
        upstream = up[h]
        cat = beside(*split(upstream * inv))
        gcat[h] = cat
        dg = -jnp.sum(upstream * out, axis=1, keepdims=True) * inv
        dgr[h] = dg
        put_state(b_own, h, to_state(phi, cat), jnp.sum(phi * dg, axis=0, keepdims=True))
        after.swap(h).start()
        return 0

    lax.fori_loop(0, H, attend, 0)

    def m_copy(r):
        return remote(m_send.at[r], m_recv.at[r], (m_sem.at[r, 0], m_sem.at[r, 1]),
                      {"head": flip_all(h_me, r)})

    order = sorted(range(n_head), reverse=True)
    mixing = []
    for r in order:
        first = pl.multiple_of(flip_all(h_me, r) * TS, TS)
        mixing.append(beside(*[att[h, pl.ds(first, TS), :] for h in range(H)]))
    mixing = jnp.concatenate(mixing, axis=0)
    step = math.gcd(D, 512)
    for c in range(0, D, step):
        part = dot(mixing, w_ref[:, c : c + step], NN)
        for i, r in enumerate(order):
            piece = part[i * TS : (i + 1) * TS]
            if r:
                m_send[r, :, c : c + step] = piece.astype(BF16)
            else:
                m_own[:, c : c + step] = piece
    for r in order:
        if r:
            m_copy(r).start()

    after.point(0)
    gcon[0:T, 0 : 2 * LANES] = jnp.zeros((T, 2 * LANES), F32)

    def query_grads(h, _):
        cat = gcat[h]
        dg = dgr[h]
        mask = mask_ref[h, 0:1, :]
        gcon[0:T, 0:HK] = gcon[0:T, 0:HK] + pull(
            on_features(cat, pf[h], dg * sums_of(pf, h)), h, aq, bq)
        for i in blocks:
            rows, width = slice(i * TB, (i + 1) * TB), (i + 1) * TB
            vh, vl = vcat[h, 0:width, :VD], vcat[h, 0:width, VD:]
            dw = dot(cat[rows], beside(vh, vh), NT) + dot(cat[rows, :VD], vl, NT) + dg[rows]
            ds = (dw * dsim[h, rows, 0:width]).astype(BF16)
            ds_buf[rows, 0:width] = ds
            gcon[rows, 0:HK] = gcon[rows, 0:HK] + fold(dot(ds, k3[0:width, : 2 * HK], NN)) * mask
        for j in blocks:
            cols = slice(j * TB, (j + 1) * TB)
            gcon[cols, LANES : LANES + HK] = gcon[cols, LANES : LANES + HK] + fold(
                dot(ds_buf[j * TB : T, cols], q2[j * TB : T, :], TN)) * mask
        return 0

    def value_local(h, _):
        for j in blocks:
            cols = slice(j * TB, (j + 1) * TB)
            gvs[h, cols, :] = fold(dot(wh[h, j * TB : T, cols], gcat[h, j * TB : T, :], TN))
        return 0

    lax.fori_loop(0, H // 2, query_grads, 0)
    after.point(1)
    lax.fori_loop(H // 2, H, query_grads, 0)
    after.point(2)
    lax.fori_loop(0, H, value_local, 0)
    after.point(3)

    def key_grads(h, _):
        dphi = on_features(vcat[h], pb[h], sums_of(pb, h))
        gcon[0:T, LANES : LANES + HK] = gcon[0:T, LANES : LANES + HK] + pull(dphi, h, ak, bk)
        gvs[h] = gvs[h] + by_state(ak[h] * bk[h], pb[h])
        return 0

    lax.fori_loop(0, H, key_grads, 0)
    for h in range(H):
        gcon[0:T, (2 + h) * LANES : (3 + h) * LANES] = gvs[h]

    tail = remote(gcon.at[pl.ds(0, RIM)], gcon.at[pl.ds(T, RIM)],
                  (halo_sem.at[1, 0], halo_sem.at[1, 1]), {"seq": prv})
    tail.start()

    grads = gcon[0:T, :]
    tr_own[...] = jnp.concatenate(
        [jnp.sum(grads * ext[RIM - j : RIM - j + T, :], axis=0, keepdims=True) for j in range(3)]
        + [jnp.zeros((5, CW), F32)], axis=0)

    def t_copy(d, at):
        return remote(tr_own, tr.at[at], (t_send.at[d], t_recv.at[at]), {"seq": (s + d) % n_seq})

    def t_start(d, _):
        t_copy(d, s).start()
        return 0

    lax.fori_loop(1, n_seq, t_start, 0)
    tr[s] = tr_own[...]

    total = m_own[...]
    for r in range(1, n_head):
        m_copy(r).wait_recv()
        total = total + m_recv[r].astype(F32)
    mixed_ref[...] = total.astype(BF16)

    tail.wait_recv()
    gcon[T : T + RIM, :] = jnp.where(s == n_seq - 1, 0.0, gcon[T : T + RIM, :])

    def conv_back(lo, hi):
        return (taps[0][:, lo:hi] * gcon[0:T, lo:hi] + taps[1][:, lo:hi] * gcon[1 : T + 1, lo:hi]
                + taps[2][:, lo:hi] * gcon[2 : T + 2, lo:hi])

    gq_ref[...] = conv_back(0, LANES).T[:HK]
    gk_ref[...] = conv_back(LANES, 2 * LANES).T[:HK]
    gv_ref[...] = conv_back(2 * LANES, CW)

    def t_wait(d, _):
        t_copy(d, (s + n_seq - d) % n_seq).wait_recv()
        return 0

    lax.fori_loop(1, n_seq, t_wait, 0)
    tap_grads = lax.fori_loop(1, n_seq, lambda j, acc: acc + tr[j], tr[0])
    gcq_ref[...] = tap_grads[0:3, 0:HK]
    gck_ref[...] = tap_grads[0:3, LANES : LANES + HK]
    gcv_ref[...] = tap_grads[0:3, 2 * LANES :]

    halo.wait_send()
    tail.wait_send()
    for _, copy in og_copies.values():
        copy.wait_send()
    for r in range(1, n_head):
        m_copy(r).wait_send()

    def t_drain(d, _):
        t_copy(d, s).wait_send()
        return 0

    lax.fori_loop(1, n_seq, t_drain, 0)
    before.drain()
    after.drain()


def solution(mesh):
    n_seq, n_head = mesh.shape["seq"], mesh.shape["head"]

    def body(query_in, key_in, value_in, conv_query, conv_key, conv_value, out_proj, out_grad):
        T, HK = query_in.shape
        VC = value_in.shape[1]
        D = out_proj.shape[1]
        H = VC // VD
        fk = HK // H
        pick, rows, mask, mask3, feat = feature_tables(fk, H)
        FL = rows.shape[1]
        FP = round_up(feat + FL // LANES, 16)
        CW = 2 * LANES + VC
        TS = T // n_head
        vmem = pl.BlockSpec(memory_space=pltpu.VMEM)
        shape = jax.ShapeDtypeStruct
        big = pltpu.VMEM
        dma = pltpu.SemaphoreType.DMA
        state = big((H, FP, VD), F32)
        mixed, gq, gk, gv, gcq, gck, gcv = pl.pallas_call(
            functools.partial(kernel, n_seq, n_head, fk, feat, FP),
            out_shape=(
                shape((TS, D), BF16), shape((HK, T), F32), shape((HK, T), F32), shape((T, VC), F32),
                shape((3, HK), F32), shape((3, HK), F32), shape((3, VC), F32),
            ),
            in_specs=[vmem] * 12,
            out_specs=tuple([vmem] * 7),
            scratch_shapes=[
                big((RIM + T, CW), F32), big((T + RIM, CW), F32),
                big((T, 3 * HK), BF16), big((T, 3 * HK), BF16), big((T, 2 * HK), BF16),
                big((H, T, 2 * VD), BF16),
                big((H, T, FL), F32), big((H, T, FL), F32), big((H, T, FL), F32), big((H, T, FL), F32),
                big((H, T, T), F32), big((H, T, T), BF16), big((T, T), BF16),
                big((H, T, VD), F32), big((H, T, 1), F32), big((H, T, VD), F32),
                big((H, T, 2 * VD), BF16), big((H, T, 1), F32), big((H, T, VD), BF16),
                big((H, T, VD), F32),
                big((n_head, TS, D), BF16), big((n_head, TS, D), BF16),
                big((n_head, TS, D), BF16), big((TS, D), F32),
                *[state] * 10,
                big((n_seq, 8, CW), F32), big((8, CW), F32),
                dma((2, 2)), dma((n_head, 2)), dma((n_head, 2)),
                dma((2, H, 2)), dma((2, H, 2)), dma((n_seq,)), dma((n_seq,)),
            ],
            compiler_params=pltpu.CompilerParams(
                collective_id=0, has_side_effects=True, vmem_limit_bytes=58 * 1024 * 1024),
        )(query_in.T, key_in.T, value_in, conv_query, conv_key, conv_value, out_proj, out_grad,
          jnp.asarray(pick), jnp.asarray(rows), jnp.asarray(mask), jnp.asarray(mask3))
        return mixed, gq.T, gk.T, gv, gcq, gck, gcv

    in_specs = (
        P("seq", "head"), P("seq", "head"), P("seq", "head"),
        P(None, "head"), P(None, "head"), P(None, "head"),
        P("head", None), P(("seq", "head"), None),
    )
    out_specs = (
        P(("seq", "head"), None), P("seq", "head"), P("seq", "head"), P("seq", "head"),
        P(None, "head"), P(None, "head"), P(None, "head"),
    )
    return jax.shard_map(body, mesh=mesh, in_specs=in_specs, out_specs=out_specs, check_vma=False)
```

time: 96.3 us -> 73.4 us (0.76)
  Pallas kernels: 82.3 us -> 63.7 us
  local copies, waits for them, and re-layouts: 11.3 us -> 7.84 us
    pallas_call x1, Pallas kernels: 82.3 us -> 63.7 us  [body(): pl.pallas_call(functools.partial(kernel, n_seq, n_head, fk, feat, FP), ou...]
    pallas_call x2 -> x0, local copies, waits for them, and re-layouts: 3.53 us -> none  [body(): pl.pallas_call(functools.partial(kernel, n_seq, n_head, fk, FP), out_shap...]
where the time goes in v1:
time: 73.4 us; the launch traced here: 72.2 us
  Pallas kernels  63.7 us (87%)
  local copies, waits for them, and re-layouts  7.84 us (11%)
    pallas_call x1, Pallas kernels, body(): pl.pallas_call(functools.partial(kernel, n_seq, n_head, fk, feat, FP), ou...  63.7 us
    unnamed x15, local copies, waits for them, and re-layouts  7.84 us

profile of v1, /device:TPU:24, one launch (start us, length us, event | category | flops | bytes accessed | tf_op | source)
XLA Modules:
  0.0 72.2 jit_solution(10543636950944056520)
XLA Ops:
  0.6 63.7 %shard_map.171 = (bf16[128,2048]{1,0:T(8,128)(2,1)}, f32[64,512]{1,0:T(8,128)}, f32[64,512]{1,0:T(8,128)}, f32[512,512]{1,0:T(8,128)}, f32[3,64]{1,0:T(4,128)}, /*index=5*/f32[3,64]{1,0:T(4,128)}, f32[3,512]{1,0:T(4,128)}) custom-call(bf16[64,512]{1,0:T(8,128)(2,1)} %bitcast.6, bf16[64,512]{1,0:T(8,128)(2,1)} %bitcast.7, bf16[512,512]{1,0:T(8,128)(2,1)} %v_ref.1, ...), custom_call_target="tpu_custom_call" | custom-call | tf_op jit(solution)/shard_map/pallas_call | solution.py:484
  64.4 0.0 copy-start
  64.4 0.0 copy-start.3
  64.4 0.0 copy-start.2
  64.4 0.0 copy-start.1
  64.4 2.0 %copy.26 = bf16[128,2048]{1,0:T(8,128)(2,1)} copy(bf16[128,2048]{1,0:T(8,128)(2,1)} %get-tuple-element.28) | data formatting | bytes 1048576
  66.4 1.6 %copy.27 = f32[512,64]{0,1:T(8,128)} copy(f32[512,64]{0,1:T(8,128)} %bitcast.5) | data formatting | bytes 262144
  67.9 1.6 %copy.28 = f32[512,64]{0,1:T(8,128)} copy(f32[512,64]{0,1:T(8,128)} %bitcast.4) | data formatting | bytes 262144
  69.5 0.0 copy-done
  69.5 1.0 %copy.29 = f32[512,512]{1,0:T(8,128)} copy(f32[512,512]{1,0:T(8,128)S(1)} %copy-done) | data formatting | bytes 2097152
  70.5 0.0 copy-done.3
  70.5 0.6 copy.30
  71.1 0.0 copy-done.2
  71.1 0.6 copy.31
  71.6 0.0 copy-done.1
  71.6 0.6 copy.32
Async XLA Ops:
  64.4 5.1 %copy-start = (f32[512,512]{1,0:T(8,128)S(1)}, f32[512,512]{1,0:T(8,128)}, u32[]{:S(2)}) copy-start(f32[512,512]{1,0:T(8,128)} %get-tuple-element.31) | copy-start | bytes 3145732
  64.4 6.1 %copy-start.3 = (f32[3,64]{1,0:T(4,128)S(1)}, f32[3,64]{1,0:T(4,128)}, u32[]{:S(2)}) copy-start(f32[3,64]{1,0:T(4,128)} %get-tuple-element.32) | copy-start | bytes 2308
  64.4 6.7 %copy-start.2 = (f32[3,64]{1,0:T(4,128)S(1)}, f32[3,64]{1,0:T(4,128)}, u32[]{:S(2)}) copy-start(f32[3,64]{1,0:T(4,128)} %get-tuple-element.33) | copy-start | bytes 2308
  64.4 7.2 %copy-start.1 = (f32[3,512]{1,0:T(4,128)S(1)}, f32[3,512]{1,0:T(4,128)}, u32[]{:S(2)}) copy-start(f32[3,512]{1,0:T(4,128)} %get-tuple-element.34) | copy-start | bytes 18436

commit v2 on v1

--- a/solution.py
+++ b/solution.py
@@ -70,11 +70,38 @@
     return x[:, :half] + x[:, half:]
 
 
+def tap_rows(cq_ref, ck_ref, cv_ref):
+    pad = jnp.zeros((1, LANES - cq_ref.shape[1]), F32)
+    return [beside(cq_ref[j : j + 1, :], pad, ck_ref[j : j + 1, :], pad, cv_ref[j : j + 1, :])
+            for j in range(3)]
+
+
+def finish(cq_ref, ck_ref, cv_ref, mixed_in, gcon, tail_ref, taps_ref,
+           mixed_ref, gq_ref, gk_ref, gv_ref, gcq_ref, gck_ref, gcv_ref):
+    T, CW = gcon.shape
+    HK = cq_ref.shape[1]
+    taps = tap_rows(cq_ref, ck_ref, cv_ref)
+
+    def conv_back(lo, hi):
+        full = jnp.concatenate([gcon[:, lo:hi], tail_ref[:, lo:hi]], axis=0)
+        return (taps[0][:, lo:hi] * full[0:T] + taps[1][:, lo:hi] * full[1 : T + 1]
+                + taps[2][:, lo:hi] * full[2 : T + 2])
+
+    mixed_ref[...] = mixed_in[...]
+    gq_ref[...] = conv_back(0, LANES).T[:HK]
+    gk_ref[...] = conv_back(LANES, 2 * LANES).T[:HK]
+    for lo in range(2 * LANES, CW, LANES):
+        gv_ref[:, lo - 2 * LANES : lo - LANES] = conv_back(lo, lo + LANES)
+    gcq_ref[...] = taps_ref[0:3, 0:HK]
+    gck_ref[...] = taps_ref[0:3, LANES : LANES + HK]
+    gcv_ref[...] = taps_ref[0:3, 2 * LANES :]
+
+
 def kernel(n_seq, n_head, fk, feat, FP,
            q_ref, k_ref, v_ref, cq_ref, ck_ref, cv_ref, w_ref, og_ref,
            pick_ref, rows_ref, mask_ref, mask3_ref,
-           mixed_ref, gq_ref, gk_ref, gv_ref, gcq_ref, gck_ref, gcv_ref,
-           ext, gcon, q3, k3, q2, vcat, aq, bq, ak, bk, dsim, wh, ds_buf,
+           mixed_ref, gcon, tail_ref, taps_ref,
+           ext, tail_buf, q3, k3, q2, vcat, aq, bq, ak, bk, dsim, wh, ds_buf,
            num, den, up, gcat, dgr, att, gvs,
            og_all, m_send, m_recv, m_own,
            f_own, f_pair, f_send, f_chain, pf, b_own, b_pair, b_send, b_chain, pb,
@@ -146,11 +173,7 @@
             copy.start()
     og_all[0] = og_ref[...]
 
-    def tap_row(j):
-        pad = jnp.zeros((1, LANES - HK), F32)
-        return beside(cq_ref[j : j + 1, :], pad, ck_ref[j : j + 1, :], pad, cv_ref[j : j + 1, :])
-
-    taps = [tap_row(j) for j in range(3)]
+    taps = tap_rows(cq_ref, ck_ref, cv_ref)
     row_a, row_b, row_c = (rows_ref[j : j + 1, :] for j in range(3))
 
     halo.wait_recv()
@@ -400,7 +423,7 @@
     for h in range(H):
         gcon[0:T, (2 + h) * LANES : (3 + h) * LANES] = gvs[h]
 
-    tail = remote(gcon.at[pl.ds(0, RIM)], gcon.at[pl.ds(T, RIM)],
+    tail = remote(gcon.at[pl.ds(0, RIM)], tail_buf,
                   (halo_sem.at[1, 0], halo_sem.at[1, 1]), {"seq": prv})
     tail.start()
 
@@ -426,25 +449,14 @@
     mixed_ref[...] = total.astype(BF16)
 
     tail.wait_recv()
-    gcon[T : T + RIM, :] = jnp.where(s == n_seq - 1, 0.0, gcon[T : T + RIM, :])
-
-    def conv_back(lo, hi):
-        return (taps[0][:, lo:hi] * gcon[0:T, lo:hi] + taps[1][:, lo:hi] * gcon[1 : T + 1, lo:hi]
-                + taps[2][:, lo:hi] * gcon[2 : T + 2, lo:hi])
-
-    gq_ref[...] = conv_back(0, LANES).T[:HK]
-    gk_ref[...] = conv_back(LANES, 2 * LANES).T[:HK]
-    gv_ref[...] = conv_back(2 * LANES, CW)
+    tail_ref[...] = jnp.where(s == n_seq - 1, 0.0, tail_buf[...])
 
     def t_wait(d, _):
         t_copy(d, (s + n_seq - d) % n_seq).wait_recv()
         return 0
 
     lax.fori_loop(1, n_seq, t_wait, 0)
-    tap_grads = lax.fori_loop(1, n_seq, lambda j, acc: acc + tr[j], tr[0])
-    gcq_ref[...] = tap_grads[0:3, 0:HK]
-    gck_ref[...] = tap_grads[0:3, LANES : LANES + HK]
-    gcv_ref[...] = tap_grads[0:3, 2 * LANES :]
+    taps_ref[...] = lax.fori_loop(1, n_seq, lambda j, acc: acc + tr[j], tr[0])
 
     halo.wait_send()
     tail.wait_send()
@@ -481,16 +493,13 @@
         big = pltpu.VMEM
         dma = pltpu.SemaphoreType.DMA
         state = big((H, FP, VD), F32)
-        mixed, gq, gk, gv, gcq, gck, gcv = pl.pallas_call(
+        mixed, gcon, tail, tap_sums = pl.pallas_call(
             functools.partial(kernel, n_seq, n_head, fk, feat, FP),
-            out_shape=(
-                shape((TS, D), BF16), shape((HK, T), F32), shape((HK, T), F32), shape((T, VC), F32),
-                shape((3, HK), F32), shape((3, HK), F32), shape((3, VC), F32),
-            ),
+            out_shape=(shape((TS, D), BF16), shape((T, CW), F32), shape((RIM, CW), F32), shape((8, CW), F32)),
             in_specs=[vmem] * 12,
-            out_specs=tuple([vmem] * 7),
+            out_specs=tuple([vmem] * 4),
             scratch_shapes=[
-                big((RIM + T, CW), F32), big((T + RIM, CW), F32),
+                big((RIM + T, CW), F32), big((RIM, CW), F32),
                 big((T, 3 * HK), BF16), big((T, 3 * HK), BF16), big((T, 2 * HK), BF16),
                 big((H, T, 2 * VD), BF16),
                 big((H, T, FL), F32), big((H, T, FL), F32), big((H, T, FL), F32), big((H, T, FL), F32),
@@ -509,6 +518,16 @@
                 collective_id=0, has_side_effects=True, vmem_limit_bytes=58 * 1024 * 1024),
         )(query_in.T, key_in.T, value_in, conv_query, conv_key, conv_value, out_proj, out_grad,
           jnp.asarray(pick), jnp.asarray(rows), jnp.asarray(mask), jnp.asarray(mask3))
+        mixed, gq, gk, gv, gcq, gck, gcv = pl.pallas_call(
+            finish,
+            out_shape=(
+                shape((TS, D), BF16), shape((HK, T), F32), shape((HK, T), F32), shape((T, VC), F32),
+                shape((3, HK), F32), shape((3, HK), F32), shape((3, VC), F32),
+            ),
+            in_specs=[vmem] * 7,
+            out_specs=tuple([vmem] * 7),
+            compiler_params=pltpu.CompilerParams(vmem_limit_bytes=58 * 1024 * 1024),
+        )(conv_query, conv_key, conv_value, mixed, gcon, tail, tap_sums)
         return mixed, gq.T, gk.T, gv, gcq, gck, gcv
 
     in_specs = (

time: 73.4 us -> 68.8 us (0.937)
  local copies, waits for them, and re-layouts: 7.84 us -> 0 us
  Pallas kernels: 63.7 us -> 67 us
    unnamed x15 -> x0, local copies, waits for them, and re-layouts: 7.84 us -> none
    pallas_call x0 -> x1, Pallas kernels: none -> 3.44 us  [body(): pl.pallas_call(finish, out_shape=(shape((TS, D), BF16), shape((HK, T), F3...]
where the time goes in v2:
time: 68.8 us; the launch traced here: 67.7 us
  Pallas kernels  67 us (97%)
    pallas_call x1, Pallas kernels, body(): pl.pallas_call(functools.partial(kernel, n_seq, n_head, fk, feat, FP), ou...  63.6 us
    pallas_call x1, Pallas kernels, body(): pl.pallas_call(finish, out_shape=(shape((TS, D), BF16), shape((HK, T), F3...  3.44 us

profile of v2, /device:TPU:24, one launch (start us, length us, event | category | flops | bytes accessed | tf_op | source)
XLA Modules:
  0.0 67.7 jit_solution(3750841199236734484)
XLA Ops:
  0.6 63.6 %shard_map.171 = (bf16[128,2048]{1,0:T(8,128)(2,1)}, f32[512,768]{1,0:T(8,128)}, f32[8,768]{1,0:T(8,128)}, f32[8,768]{1,0:T(8,128)}) custom-call(bf16[64,512]{1,0:T(8,128)(2,1)} %bitcast.4, bf16[64,512]{1,0:T(8,128)(2,1)} %bitcast.5, bf16[512,512]{1,0:T(8,128)(2,1)} %v_ref.1, f32[3,64]{1,0:T(4,128)} %cq_ref.3, f32[3,64]{1,0:T(4,128)} %ck_ref.3, ...), custom_call_target="tpu_custom_call" | custom-call | tf_op jit(solution)/shard_map/pallas_call | solution.py:496
  64.3 3.4 %shard_map.172 = (bf16[128,2048]{1,0:T(8,128)(2,1)}, f32[64,512]{1,0:T(8,128)}, f32[64,512]{1,0:T(8,128)}, f32[512,512]{1,0:T(8,128)}, f32[3,64]{1,0:T(4,128)}, /*index=5*/f32[3,64]{1,0:T(4,128)}, f32[3,512]{1,0:T(4,128)}) custom-call(f32[3,64]{1,0:T(4,128)} %cq_ref.3, f32[3,64]{1,0:T(4,128)} %ck_ref.3, f32[3,512]{1,0:T(4,128)} %cv_ref.3, ...), custom_call_target="tpu_custom_call" | custom-call | tf_op jit(solution)/shard_map/pallas_call | solution.py:521

commit v3 on v2

--- a/solution.py
+++ b/solution.py
@@ -98,15 +98,15 @@
 
 
 def kernel(n_seq, n_head, fk, feat, FP,
-           q_ref, k_ref, v_ref, cq_ref, ck_ref, cv_ref, w_ref, og_ref,
+           q_ref, k_ref, v_ref, cq_ref, ck_ref, cv_ref, w_hbm, og_ref,
            pick_ref, rows_ref, mask_ref, mask3_ref,
            mixed_ref, gcon, tail_ref, taps_ref,
            ext, tail_buf, q3, k3, q2, vcat, aq, bq, ak, bk, dsim, wh, ds_buf,
            num, den, up, gcat, dgr, att, gvs,
            og_all, m_send, m_recv, m_own,
-           f_own, f_pair, f_send, f_chain, pf, b_own, b_pair, b_send, b_chain, pb,
-           tr, tr_own,
-           halo_sem, og_sem, m_sem, f_sem, b_sem, t_send, t_recv):
+           f_own, f_pair, f_send, f_chain, f_back, pf, b_own, b_pair, b_send, b_chain, b_back, pb,
+           tr, tr_own, taps_buf, w_ref,
+           halo_sem, og_sem, m_sem, f_sem, b_sem, t_send, t_recv, w_sem):
     HK, T = q_ref.shape
     VC = v_ref.shape[1]
     D = w_ref.shape[1]
@@ -134,6 +134,8 @@
     prv = (s + n_seq - 1) % n_seq
 
     barrier = pltpu.get_barrier_semaphore()
+    load_w = pltpu.make_async_copy(w_hbm, w_ref, w_sem)
+    load_w.start()
 
     def greet(d, _):
         pl.semaphore_signal(barrier, inc=1, device_id={"seq": (s + d) % n_seq}, device_id_type=MESH)
@@ -174,6 +176,8 @@
     og_all[0] = og_ref[...]
 
     taps = tap_rows(cq_ref, ck_ref, cv_ref)
+    for j in range(3):
+        taps_buf[j : j + 1, :] = taps[j]
     row_a, row_b, row_c = (rows_ref[j : j + 1, :] for j in range(3))
 
     halo.wait_recv()
@@ -186,16 +190,20 @@
 
     high, low = split(conv(LANES, 2 * LANES)[:, :HK])
     k3[...] = beside(high, low, high)
-    for h in range(H):
-        vcat[h] = beside(*split(conv((2 + h) * LANES, (3 + h) * LANES)))
 
     def put_state(buf, h, state, total):
-        buf[h, :, :] = state
+        buf[h, 0, :, :] = state[: FP // 2]
+        buf[h, 1, :, :] = state[FP // 2 :]
         for c in range(FL // LANES):
-            buf[h, feat + c : feat + c + 1, :] = total[:, c * LANES : (c + 1) * LANES]
+            half, row = divmod(feat + c, FP // 2)
+            buf[h, half, row : row + 1, :] = total[:, c * LANES : (c + 1) * LANES]
+
+    def state_of(buf, h):
+        return jnp.concatenate([buf[h, 0], buf[h, 1]], axis=0)
 
     def sums_of(buf, h):
-        return beside(*[buf[h, feat + c : feat + c + 1, :] for c in range(FL // LANES)])
+        rows = [divmod(feat + c, FP // 2) for c in range(FL // LANES)]
+        return beside(*[buf[h, half, row : row + 1, :] for half, row in rows])
 
     def factors(x2, h, a_buf, b_buf):
         both = dot(x2, pick_ref[h], NN)
@@ -224,20 +232,24 @@
         return beside(dphi, jnp.zeros((T, FL - FP), F32)) + total
 
     class Scan:
-        def __init__(self, own, pair_buf, send, chain, total, sem, later):
+        def __init__(self, own, pair_buf, send, chain, back, total, sem, later):
             self.own, self.pair_buf, self.send, self.chain = own, pair_buf, send, chain
-            self.total, self.sem, self.later = total, sem, later
+            self.back, self.total, self.sem = back, total, sem
             self.place = Z - 1 - z if later else z
             self.wanted = odd == (0 if later else 1)
             self.target = (s + n_seq - 2) % n_seq if later else (s + 2) % n_seq
 
+        def link(self, i, h, src, dst, to):
+            return remote(src, dst, (self.sem.at[i, h, 0], self.sem.at[i, h, 1]), {"seq": to})
+
         def swap(self, h):
-            return remote(self.own.at[h], self.pair_buf.at[h],
-                          (self.sem.at[0, h, 0], self.sem.at[0, h, 1]), {"seq": pair})
+            return self.link(0, h, self.own.at[h, 1 - odd], self.pair_buf.at[h], pair)
 
         def pass_on(self, h):
-            return remote(self.send.at[h], self.chain.at[h],
-                          (self.sem.at[1, h, 0], self.sem.at[1, h, 1]), {"seq": self.target})
+            return self.link(1, h, self.send.at[h], self.chain.at[h], self.target)
+
+        def give_back(self, h):
+            return self.link(2, h, self.back.at[h], self.total.at[h, odd], pair)
 
         def point(self, p):
             if p >= Z:
@@ -246,12 +258,19 @@
                 def one(h, _):
                     self.swap(h).wait_recv()
                     arrived = self.pair_buf[h]
-                    self.total[h] = jnp.where(self.wanted, arrived, 0.0)
-                    self.send[h] = self.own[h] + arrived
+                    mine = self.own[h, odd]
+                    self.send[h] = mine + arrived
                     if Z > 1:
                         @pl.when(self.place == 0)
                         def _():
                             self.pass_on(h).start()
+                    self.total[h, odd] = jnp.where(self.wanted, arrived, 0.0)
+                    self.back[h] = jnp.where(self.wanted, 0.0, mine)
+
+                    @pl.when(self.place == 0)
+                    def _():
+                        self.give_back(h).start()
+
                     return 0
 
                 lax.fori_loop(0, H, one, 0)
@@ -268,14 +287,20 @@
                         self.send[h] = self.send[h] + arrived
                         self.pass_on(h).start()
 
-                    self.total[h] = self.total[h] + arrived
+                    self.back[h] = self.back[h] + arrived
+                    self.give_back(h).start()
+                    self.total[h, odd] = self.total[h, odd] + arrived
                     return 0
 
                 lax.fori_loop(0, H, one, 0)
+
+        def ready(self, h):
+            self.give_back(h).wait_recv()
 
         def drain(self):
             def one(h, _):
                 self.swap(h).wait_send()
+                self.give_back(h).wait_send()
 
                 @pl.when(self.place < Z - 1)
                 def _():
@@ -285,11 +310,14 @@
 
             lax.fori_loop(0, H, one, 0)
 
-    before = Scan(f_own, f_pair, f_send, f_chain, pf, f_sem, False)
-    after = Scan(b_own, b_pair, b_send, b_chain, pb, b_sem, True)
+    before = Scan(f_own, f_pair, f_send, f_chain, f_back, pf, f_sem, False)
+    after = Scan(b_own, b_pair, b_send, b_chain, b_back, pb, b_sem, True)
 
     def key_side(h, _):
         phi = factors(k3[:, : 2 * HK], h, ak, bk)
+        lanes = pl.ds(pl.multiple_of((2 + h) * LANES, LANES), LANES)
+        value = sum(taps_buf[j : j + 1, lanes] * ext[pl.ds(RIM - j, T), lanes] for j in range(3))
+        vcat[h] = beside(*split(value))
         put_state(f_own, h, to_state(phi, vcat[h]), jnp.sum(phi, axis=0, keepdims=True))
         before.swap(h).start()
         return 0
@@ -331,6 +359,7 @@
     for r in held:
         if r != 0 and r not in forwarded:
             og_copies[r][1].wait_recv()
+    load_w.wait()
     for h in range(H):
         product = dot(og_all[...].reshape(T, D), w_ref[h * VD : (h + 1) * VD, :], NT)
         for r in range(n_head):
@@ -340,9 +369,10 @@
 
     def attend(h, _):
         phi = aq[h] * bq[h]
+        before.ready(h)
         denom = den[h] + jnp.sum(phi * sums_of(pf, h), axis=1, keepdims=True)
         inv = 1.0 / denom
-        out = (num[h] + by_state(phi, pf[h])) * inv
+        out = (num[h] + by_state(phi, state_of(pf, h))) * inv
         att[h] = out.astype(BF16)
         upstream = up[h]
         cat = beside(*split(upstream * inv))
@@ -386,7 +416,7 @@
         dg = dgr[h]
         mask = mask_ref[h, 0:1, :]
         gcon[0:T, 0:HK] = gcon[0:T, 0:HK] + pull(
-            on_features(cat, pf[h], dg * sums_of(pf, h)), h, aq, bq)
+            on_features(cat, state_of(pf, h), dg * sums_of(pf, h)), h, aq, bq)
         for i in blocks:
             rows, width = slice(i * TB, (i + 1) * TB), (i + 1) * TB
             vh, vl = vcat[h, 0:width, :VD], vcat[h, 0:width, VD:]
@@ -414,9 +444,10 @@
     after.point(3)
 
     def key_grads(h, _):
-        dphi = on_features(vcat[h], pb[h], sums_of(pb, h))
+        after.ready(h)
+        dphi = on_features(vcat[h], state_of(pb, h), sums_of(pb, h))
         gcon[0:T, LANES : LANES + HK] = gcon[0:T, LANES : LANES + HK] + pull(dphi, h, ak, bk)
-        gvs[h] = gvs[h] + by_state(ak[h] * bk[h], pb[h])
+        gvs[h] = gvs[h] + by_state(ak[h] * bk[h], state_of(pb, h))
         return 0
 
     lax.fori_loop(0, H, key_grads, 0)
@@ -492,11 +523,11 @@
         shape = jax.ShapeDtypeStruct
         big = pltpu.VMEM
         dma = pltpu.SemaphoreType.DMA
-        state = big((H, FP, VD), F32)
+        state, half = big((H, 2, FP // 2, VD), F32), big((H, FP // 2, VD), F32)
         mixed, gcon, tail, tap_sums = pl.pallas_call(
             functools.partial(kernel, n_seq, n_head, fk, feat, FP),
             out_shape=(shape((TS, D), BF16), shape((T, CW), F32), shape((RIM, CW), F32), shape((8, CW), F32)),
-            in_specs=[vmem] * 12,
+            in_specs=[vmem] * 6 + [pl.BlockSpec(memory_space=pl.ANY)] + [vmem] * 5,
             out_specs=tuple([vmem] * 4),
             scratch_shapes=[
                 big((RIM + T, CW), F32), big((RIM, CW), F32),
@@ -509,10 +540,10 @@
                 big((H, T, VD), F32),
                 big((n_head, TS, D), BF16), big((n_head, TS, D), BF16),
                 big((n_head, TS, D), BF16), big((TS, D), F32),
-                *[state] * 10,
-                big((n_seq, 8, CW), F32), big((8, CW), F32),
+                *[state, half, half, half, half, state] * 2,
+                big((n_seq, 8, CW), F32), big((8, CW), F32), big((8, CW), F32), big((VC, D), BF16),
                 dma((2, 2)), dma((n_head, 2)), dma((n_head, 2)),
-                dma((2, H, 2)), dma((2, H, 2)), dma((n_seq,)), dma((n_seq,)),
+                dma((3, H, 2)), dma((3, H, 2)), dma((n_seq,)), dma((n_seq,)), pltpu.SemaphoreType.DMA(()),
             ],
             compiler_params=pltpu.CompilerParams(
                 collective_id=0, has_side_effects=True, vmem_limit_bytes=58 * 1024 * 1024),

time: 68.8 us -> 59.3 us (0.86); the launches traced: 67.7 us -> 59.2 us
  Pallas kernels: 67 us -> 58.5 us
    pallas_call x1, Pallas kernels: 63.6 us -> 55.1 us  [body(): pl.pallas_call(functools.partial(kernel, n_seq, n_head, fk, feat, FP), ou...]
where the time goes in v3:
time: 59.3 us; the launch traced here: 59.2 us
  Pallas kernels  58.5 us (99%)
  between operations  0.64 us (1%)
    pallas_call x1, Pallas kernels, body(): pl.pallas_call(functools.partial(kernel, n_seq, n_head, fk, feat, FP), ou...  55.1 us
    pallas_call x1, Pallas kernels, body(): pl.pallas_call(finish, out_shape=(shape((TS, D), BF16), shape((HK, T), F3...  3.44 us

profile of v3, /device:TPU:24, one launch (start us, length us, event | category | flops | bytes accessed | tf_op | source)
XLA Modules:
  0.0 59.2 jit_solution(8228663776685184522)
XLA Ops:
  0.6 55.1 %shard_map.171 = (bf16[128,2048]{1,0:T(8,128)(2,1)}, f32[512,768]{1,0:T(8,128)}, f32[8,768]{1,0:T(8,128)}, f32[8,768]{1,0:T(8,128)}) custom-call(bf16[64,512]{1,0:T(8,128)(2,1)} %bitcast.4, bf16[64,512]{1,0:T(8,128)(2,1)} %bitcast.5, bf16[512,512]{1,0:T(8,128)(2,1)} %v_ref.1, f32[3,64]{1,0:T(4,128)} %cq_ref.3, f32[3,64]{1,0:T(4,128)} %ck_ref.3, ...), custom_call_target="tpu_custom_call" | custom-call | tf_op jit(solution)/shard_map/pallas_call | solution.py:527
  55.7 3.4 %shard_map.172 = (bf16[128,2048]{1,0:T(8,128)(2,1)}, f32[64,512]{1,0:T(8,128)}, f32[64,512]{1,0:T(8,128)}, f32[512,512]{1,0:T(8,128)}, f32[3,64]{1,0:T(4,128)}, /*index=5*/f32[3,64]{1,0:T(4,128)}, f32[3,512]{1,0:T(4,128)}) custom-call(f32[3,64]{1,0:T(4,128)} %cq_ref.3, f32[3,64]{1,0:T(4,128)} %ck_ref.3, f32[3,512]{1,0:T(4,128)} %cv_ref.3, ...), custom_call_target="tpu_custom_call" | custom-call | tf_op jit(solution)/shard_map/pallas_call | solution.py:552

commit v4 on v3

--- a/solution.py
+++ b/solution.py
@@ -101,7 +101,7 @@
            q_ref, k_ref, v_ref, cq_ref, ck_ref, cv_ref, w_hbm, og_ref,
            pick_ref, rows_ref, mask_ref, mask3_ref,
            mixed_ref, gcon, tail_ref, taps_ref,
-           ext, tail_buf, q3, k3, q2, vcat, aq, bq, ak, bk, dsim, wh, ds_buf,
+           ext, rim, tail_buf, q3, k3, q2, vcat, aq, bq, ak, bk, dsim, draw, wh, ds_buf,
            num, den, up, gcat, dgr, att, gvs,
            og_all, m_send, m_recv, m_own,
            f_own, f_pair, f_send, f_chain, f_back, pf, b_own, b_pair, b_send, b_chain, b_back, pb,
@@ -145,10 +145,13 @@
     for r in range(1, n_head):
         pl.semaphore_signal(barrier, inc=1, device_id={"head": flip_all(h_me, r)}, device_id_type=MESH)
 
-    zero_rows = jnp.zeros((LANES - HK, T), F32)
-    ext[RIM:, 0:LANES] = jnp.concatenate([q_ref[...].astype(F32), zero_rows], axis=0).T
-    ext[RIM:, LANES : 2 * LANES] = jnp.concatenate([k_ref[...].astype(F32), zero_rows], axis=0).T
-    ext[RIM:, 2 * LANES :] = v_ref[...].astype(F32)
+    def upright(block):
+        pad = jnp.zeros((LANES - HK, block.shape[1]), F32)
+        return jnp.concatenate([block.astype(F32), pad], axis=0).T
+
+    rim[:, 0:LANES] = upright(q_ref[:, T - LANES :])[LANES - RIM :]
+    rim[:, LANES : 2 * LANES] = upright(k_ref[:, T - LANES :])[LANES - RIM :]
+    rim[:, 2 * LANES :] = v_ref[T - 16 :, :].astype(F32)[16 - RIM :]
 
     pl.semaphore_wait(barrier, n_seq - 1 + n_head - 1)
 
@@ -157,7 +160,7 @@
             src_ref=src, dst_ref=dst, send_sem=sem[0], recv_sem=sem[1],
             device_id=where, device_id_type=MESH)
 
-    halo = remote(ext.at[pl.ds(T, RIM)], ext.at[pl.ds(0, RIM)],
+    halo = remote(rim, ext.at[pl.ds(0, RIM)],
                   (halo_sem.at[0, 0], halo_sem.at[0, 1]), {"seq": nxt})
     halo.start()
 
@@ -173,6 +176,9 @@
     for r, (src, copy) in og_copies.items():
         if src == 0:
             copy.start()
+    ext[RIM:, 0:LANES] = upright(q_ref[...])
+    ext[RIM:, LANES : 2 * LANES] = upright(k_ref[...])
+    ext[RIM:, 2 * LANES :] = v_ref[...].astype(F32)
     og_all[0] = og_ref[...]
 
     taps = tap_rows(cq_ref, ck_ref, cv_ref)
@@ -365,6 +371,17 @@
         for r in range(n_head):
             first = pl.multiple_of(flip_all(h_me, r) * TS, TS)
             up[h, pl.ds(first, TS), :] = product[r * TS : (r + 1) * TS]
+
+    def weight_grads(h, _):
+        cat = beside(*split(up[h]))
+        for i in blocks:
+            rows, width = slice(i * TB, (i + 1) * TB), (i + 1) * TB
+            vh, vl = vcat[h, 0:width, :VD], vcat[h, 0:width, VD:]
+            draw[h, rows, 0:width] = (dot(cat[rows], beside(vh, vh), NT)
+                                      + dot(cat[rows, :VD], vl, NT))
+        return 0
+
+    lax.fori_loop(0, H, weight_grads, 0)
     before.point(3)
 
     def attend(h, _):
@@ -372,6 +389,7 @@
         before.ready(h)
         denom = den[h] + jnp.sum(phi * sums_of(pf, h), axis=1, keepdims=True)
         inv = 1.0 / denom
+        den[h] = inv
         out = (num[h] + by_state(phi, state_of(pf, h))) * inv
         att[h] = out.astype(BF16)
         upstream = up[h]
@@ -387,7 +405,15 @@
 
     def m_copy(r):
         return remote(m_send.at[r], m_recv.at[r], (m_sem.at[r, 0], m_sem.at[r, 1]),
-                      {"head": flip_all(h_me, r)})
+                      {"head": flip_all(h_me, r & -r)})
+
+    def m_take(b):
+        for r in range(0, n_head, 2 * b):
+            m_copy(r + b).wait_recv()
+            m_own[r // 2] = m_own[r // 2] + m_recv[r + b].astype(F32)
+        for r in range(2 * b, n_head, 4 * b):
+            m_send[r] = m_own[r // 2].astype(BF16)
+            m_copy(r).start()
 
     order = sorted(range(n_head), reverse=True)
     mixing = []
@@ -400,12 +426,12 @@
         part = dot(mixing, w_ref[:, c : c + step], NN)
         for i, r in enumerate(order):
             piece = part[i * TS : (i + 1) * TS]
-            if r:
+            if r % 2:
                 m_send[r, :, c : c + step] = piece.astype(BF16)
             else:
-                m_own[:, c : c + step] = piece
+                m_own[r // 2, :, c : c + step] = piece
     for r in order:
-        if r:
+        if r % 2:
             m_copy(r).start()
 
     after.point(0)
@@ -419,8 +445,7 @@
             on_features(cat, state_of(pf, h), dg * sums_of(pf, h)), h, aq, bq)
         for i in blocks:
             rows, width = slice(i * TB, (i + 1) * TB), (i + 1) * TB
-            vh, vl = vcat[h, 0:width, :VD], vcat[h, 0:width, VD:]
-            dw = dot(cat[rows], beside(vh, vh), NT) + dot(cat[rows, :VD], vl, NT) + dg[rows]
+            dw = draw[h, rows, 0:width] * den[h, rows, :] + dg[rows]
             ds = (dw * dsim[h, rows, 0:width]).astype(BF16)
             ds_buf[rows, 0:width] = ds
             gcon[rows, 0:HK] = gcon[rows, 0:HK] + fold(dot(ds, k3[0:width, : 2 * HK], NN)) * mask
@@ -436,7 +461,10 @@
             gvs[h, cols, :] = fold(dot(wh[h, j * TB : T, cols], gcat[h, j * TB : T, :], TN))
         return 0
 
-    lax.fori_loop(0, H // 2, query_grads, 0)
+    head_bits = [1 << i for i in range(n_head.bit_length() - 1)]
+    lax.fori_loop(0, H // 4, query_grads, 0)
+    m_take(head_bits[0])
+    lax.fori_loop(H // 4, H // 2, query_grads, 0)
     after.point(1)
     lax.fori_loop(H // 2, H, query_grads, 0)
     after.point(2)
@@ -473,11 +501,9 @@
     lax.fori_loop(1, n_seq, t_start, 0)
     tr[s] = tr_own[...]
 
-    total = m_own[...]
-    for r in range(1, n_head):
-        m_copy(r).wait_recv()
-        total = total + m_recv[r].astype(F32)
-    mixed_ref[...] = total.astype(BF16)
+    for b in head_bits[1:]:
+        m_take(b)
+    mixed_ref[...] = m_own[0].astype(BF16)
 
     tail.wait_recv()
     tail_ref[...] = jnp.where(s == n_seq - 1, 0.0, tail_buf[...])
@@ -530,16 +556,16 @@
             in_specs=[vmem] * 6 + [pl.BlockSpec(memory_space=pl.ANY)] + [vmem] * 5,
             out_specs=tuple([vmem] * 4),
             scratch_shapes=[
-                big((RIM + T, CW), F32), big((RIM, CW), F32),
+                big((RIM + T, CW), F32), big((RIM, CW), F32), big((RIM, CW), F32),
                 big((T, 3 * HK), BF16), big((T, 3 * HK), BF16), big((T, 2 * HK), BF16),
                 big((H, T, 2 * VD), BF16),
                 big((H, T, FL), F32), big((H, T, FL), F32), big((H, T, FL), F32), big((H, T, FL), F32),
-                big((H, T, T), F32), big((H, T, T), BF16), big((T, T), BF16),
+                big((H, T, T), F32), big((H, T, T), F32), big((H, T, T), BF16), big((T, T), BF16),
                 big((H, T, VD), F32), big((H, T, 1), F32), big((H, T, VD), F32),
                 big((H, T, 2 * VD), BF16), big((H, T, 1), F32), big((H, T, VD), BF16),
                 big((H, T, VD), F32),
                 big((n_head, TS, D), BF16), big((n_head, TS, D), BF16),
-                big((n_head, TS, D), BF16), big((TS, D), F32),
+                big((n_head, TS, D), BF16), big((n_head // 2, TS, D), F32),
                 *[state, half, half, half, half, state] * 2,
                 big((n_seq, 8, CW), F32), big((8, CW), F32), big((8, CW), F32), big((VC, D), BF16),
                 dma((2, 2)), dma((n_head, 2)), dma((n_head, 2)),

time: 59.3 us -> 58.7 us (0.990); the launches traced: 59.2 us -> 57.7 us
  Pallas kernels: 58.5 us -> 57 us
    pallas_call x1, Pallas kernels: 55.1 us -> 53.6 us  [body(): pl.pallas_call(functools.partial(kernel, n_seq, n_head, fk, feat, FP), ou...]
where the time goes in v4:
time: 58.7 us; the launch traced here: 57.7 us
  Pallas kernels  57 us (97%)
  between operations  0.64 us (1%)
    pallas_call x1, Pallas kernels, body(): pl.pallas_call(functools.partial(kernel, n_seq, n_head, fk, feat, FP), ou...  53.6 us
    pallas_call x1, Pallas kernels, body(): pl.pallas_call(finish, out_shape=(shape((TS, D), BF16), shape((HK, T), F3...  3.44 us

profile of v4, /device:TPU:24, one launch (start us, length us, event | category | flops | bytes accessed | tf_op | source)
XLA Modules:
  0.0 57.7 jit_solution(17422727041397819523)
XLA Ops:
  0.6 53.6 %shard_map.171 = (bf16[128,2048]{1,0:T(8,128)(2,1)}, f32[512,768]{1,0:T(8,128)}, f32[8,768]{1,0:T(8,128)}, f32[8,768]{1,0:T(8,128)}) custom-call(bf16[64,512]{1,0:T(8,128)(2,1)} %bitcast.4, bf16[64,512]{1,0:T(8,128)(2,1)} %bitcast.5, bf16[512,512]{1,0:T(8,128)(2,1)} %v_ref.1, f32[3,64]{1,0:T(4,128)} %cq_ref.3, f32[3,64]{1,0:T(4,128)} %ck_ref.3, ...), custom_call_target="tpu_custom_call" | custom-call | tf_op jit(solution)/shard_map/pallas_call | solution.py:553
  54.2 3.4 %shard_map.172 = (bf16[128,2048]{1,0:T(8,128)(2,1)}, f32[64,512]{1,0:T(8,128)}, f32[64,512]{1,0:T(8,128)}, f32[512,512]{1,0:T(8,128)}, f32[3,64]{1,0:T(4,128)}, /*index=5*/f32[3,64]{1,0:T(4,128)}, f32[3,512]{1,0:T(4,128)}) custom-call(f32[3,64]{1,0:T(4,128)} %cq_ref.3, f32[3,64]{1,0:T(4,128)} %ck_ref.3, f32[3,512]{1,0:T(4,128)} %cv_ref.3, ...), custom_call_target="tpu_custom_call" | custom-call | tf_op jit(solution)/shard_map/pallas_call | solution.py:578

commit v5 on v4

--- a/solution.py
+++ b/solution.py
@@ -328,7 +328,7 @@
         before.swap(h).start()
         return 0
 
-    lax.fori_loop(0, H, key_side, 0)
+    lax.fori_loop(0, H, key_side, 0, unroll=True)
 
     high, low = split(conv(0, LANES)[:, :HK])
     q3[...] = beside(high, high, low)
@@ -350,11 +350,11 @@
         return 0
 
     cuts = [0, H // 2, H - H // 4, H]
-    lax.fori_loop(cuts[0], cuts[1], query_side, 0)
+    lax.fori_loop(cuts[0], cuts[1], query_side, 0, unroll=True)
     before.point(0)
-    lax.fori_loop(cuts[1], cuts[2], query_side, 0)
+    lax.fori_loop(cuts[1], cuts[2], query_side, 0, unroll=True)
     before.point(1)
-    lax.fori_loop(cuts[2], cuts[3], query_side, 0)
+    lax.fori_loop(cuts[2], cuts[3], query_side, 0, unroll=True)
     for r, (src, copy) in og_copies.items():
         if src != 0:
             og_copies[src][1].wait_recv()
@@ -381,7 +381,7 @@
                                       + dot(cat[rows, :VD], vl, NT))
         return 0
 
-    lax.fori_loop(0, H, weight_grads, 0)
+    lax.fori_loop(0, H, weight_grads, 0, unroll=True)
     before.point(3)
 
     def attend(h, _):
@@ -401,7 +401,7 @@
         after.swap(h).start()
         return 0
 
-    lax.fori_loop(0, H, attend, 0)
+    lax.fori_loop(0, H, attend, 0, unroll=True)
 
     def m_copy(r):
         return remote(m_send.at[r], m_recv.at[r], (m_sem.at[r, 0], m_sem.at[r, 1]),
@@ -462,13 +462,13 @@
         return 0
 
     head_bits = [1 << i for i in range(n_head.bit_length() - 1)]
-    lax.fori_loop(0, H // 4, query_grads, 0)
+    lax.fori_loop(0, H // 4, query_grads, 0, unroll=True)
     m_take(head_bits[0])
-    lax.fori_loop(H // 4, H // 2, query_grads, 0)
+    lax.fori_loop(H // 4, H // 2, query_grads, 0, unroll=True)
     after.point(1)
-    lax.fori_loop(H // 2, H, query_grads, 0)
+    lax.fori_loop(H // 2, H, query_grads, 0, unroll=True)
     after.point(2)
-    lax.fori_loop(0, H, value_local, 0)
+    lax.fori_loop(0, H, value_local, 0, unroll=True)
     after.point(3)
 
     def key_grads(h, _):
@@ -478,7 +478,7 @@
         gvs[h] = gvs[h] + by_state(ak[h] * bk[h], state_of(pb, h))
         return 0
 
-    lax.fori_loop(0, H, key_grads, 0)
+    lax.fori_loop(0, H, key_grads, 0, unroll=True)
     for h in range(H):
         gcon[0:T, (2 + h) * LANES : (3 + h) * LANES] = gvs[h]
 

time: 58.7 us -> 58.8 us (level)
  no operation moved by 1% of the time
where the time goes in v5:
time: 58.8 us; the launch traced here: 57.8 us
  Pallas kernels  57.1 us (97%)
  between operations  0.64 us (1%)
    pallas_call x1, Pallas kernels, body(): pl.pallas_call(functools.partial(kernel, n_seq, n_head, fk, feat, FP), ou...  53.7 us
    pallas_call x1, Pallas kernels, body(): pl.pallas_call(finish, out_shape=(shape((TS, D), BF16), shape((HK, T), F3...  3.44 us

profile of v5, /device:TPU:24, one launch (start us, length us, event | category | flops | bytes accessed | tf_op | source)
XLA Modules:
  0.0 57.8 jit_solution(4226925206274516061)
XLA Ops:
  0.6 53.7 %shard_map.171 = (bf16[128,2048]{1,0:T(8,128)(2,1)}, f32[512,768]{1,0:T(8,128)}, f32[8,768]{1,0:T(8,128)}, f32[8,768]{1,0:T(8,128)}) custom-call(bf16[64,512]{1,0:T(8,128)(2,1)} %bitcast.4, bf16[64,512]{1,0:T(8,128)(2,1)} %bitcast.5, bf16[512,512]{1,0:T(8,128)(2,1)} %v_ref.1, f32[3,64]{1,0:T(4,128)} %cq_ref.3, f32[3,64]{1,0:T(4,128)} %ck_ref.3, ...), custom_call_target="tpu_custom_call" | custom-call | tf_op jit(solution)/shard_map/pallas_call | solution.py:553
  54.3 3.4 %shard_map.172 = (bf16[128,2048]{1,0:T(8,128)(2,1)}, f32[64,512]{1,0:T(8,128)}, f32[64,512]{1,0:T(8,128)}, f32[512,512]{1,0:T(8,128)}, f32[3,64]{1,0:T(4,128)}, /*index=5*/f32[3,64]{1,0:T(4,128)}, f32[3,512]{1,0:T(4,128)}) custom-call(f32[3,64]{1,0:T(4,128)} %cq_ref.3, f32[3,64]{1,0:T(4,128)} %ck_ref.3, f32[3,512]{1,0:T(4,128)} %cv_ref.3, ...), custom_call_target="tpu_custom_call" | custom-call | tf_op jit(solution)/shard_map/pallas_call | solution.py:578
